TPU v7x, 256 devices: a whole 4x4x8 slice. The times are simulated.
256 devices in a mesh: row: 16 (over x_lo, y, core), col: 16 (over z, x_hi).
Axes of the slice: x: 4 (x_hi: 2, x_lo: 2; x = x_hi * 2 + x_lo), y: 4, z: 8, core: 2. Of those that a mesh axis runs over, the one named last changes fastest.
Arguments:
- inputs: bfloat16 [640, 12288], P('col', 'row'), may hold values from -6 to 6
- w_first: bfloat16 [12288, 49152], P('row', 'col'), may hold values from -0.0546875 to 0.0546875
- w_second: bfloat16 [49152, 12288], P('col', 'row'), may hold values from -0.02734375 to 0.02734375
- grad_out: bfloat16 [640, 12288], P('col', 'row'), may hold values from -6 to 6
Outputs:
- outputs: float32 [640, 12288], P('col', 'row')
- grad_in: float32 [640, 12288], P('col', 'row')
All inputs are finite; a program needn't handle non-finite values.
Results may differ from a plain program's by a relative error of at most 0.0029.
Values may be sent and summed in bfloat16 or wider, within the bound.
A program may use at most 128 MiB of HBM per device.

v0:
```python
import jax
import jax.numpy as jnp
from jax import lax
from jax.sharding import PartitionSpec as P

coef_a = 0.7978845608
coef_b = 0.044715


def gelu_value(h):
    t = jnp.tanh(coef_a * (h + coef_b * h * h * h))
    return 0.5 * h * (1.0 + t)


def gelu_slope(h):
    t = jnp.tanh(coef_a * (h + coef_b * h * h * h))
    return 0.5 * (1.0 + t) + 0.5 * h * (1.0 - t * t) * coef_a * (1.0 + 3.0 * coef_b * h * h)


def rows_times(panel, weight):
    return jnp.dot(panel, weight, preferred_element_type=jnp.float32)


def rows_times_transposed(panel, weight):
    return lax.dot_general(
        panel, weight, (((1,), (1,)), ((), ())), preferred_element_type=jnp.float32
    )


def on_device(inputs, w_first, w_second, grad_out):
    input_full = lax.all_gather(inputs, "col", axis=0, tiled=True)
    hidden = lax.psum_scatter(
        rows_times(input_full, w_first), "row", scatter_dimension=0, tiled=True
    )
    activated = gelu_value(hidden).astype(jnp.bfloat16)
    activated_full = lax.all_gather(activated, "row", axis=0, tiled=True)
    outputs = lax.psum_scatter(
        rows_times(activated_full, w_second), "col", scatter_dimension=0, tiled=True
    )
    cotangent_full = lax.all_gather(grad_out, "col", axis=0, tiled=True)
    grad_act = lax.psum_scatter(
        rows_times_transposed(cotangent_full, w_second), "row", scatter_dimension=0, tiled=True
    )
    grad_hidden = (grad_act * gelu_slope(hidden)).astype(jnp.bfloat16)
    grad_hidden_full = lax.all_gather(grad_hidden, "row", axis=0, tiled=True)
    grad_in = lax.psum_scatter(
        rows_times_transposed(grad_hidden_full, w_first), "col", scatter_dimension=0, tiled=True
    )
    return (outputs, grad_in)


def solution(mesh):
    in_specs = (P("col", "row"), P("row", "col"), P("col", "row"), P("col", "row"))
    out_specs = (P("col", "row"), P("col", "row"))
    return jax.shard_map(
        on_device, mesh=mesh, in_specs=in_specs, out_specs=out_specs, check_vma=False
    )
```

profile of v0, /device:TPU:8, one launch (start us, length us, event | category | flops | bytes accessed | tf_op | source)
XLA Modules:
  0.0 733.8 jit_solution(15837605802594771448)
XLA Ops:
  7.2 0.0 reduce-scatter.5.cloned.1.call-start
  7.2 50.5 %all_gather.12 = bf16[640,768]{1,0:T(8,128)(2,1)S(1)} all-gather(bf16[40,768]{1,0:T(8,128)(2,1)} %param.4), channel_id=1, replica_groups=mesh['row'=16,'col'=16] {'col'}, dimensions={0}, use_global_device_ids=true | all-gather | bytes 1044480 | tf_op jit(solution)/shard_map/all_gather | solution.py:31
  57.7 7.7 %fusion.7 = f32[640,3072]{1,0:T(8,128)} fusion(bf16[640,768]{1,0:T(8,128)(2,1)S(1)} %all_gather.12, bf16[768,3072]{1,0:T(8,128)(2,1)} %param.5), kind=kOutput, calls=%fused_computation.10 | convolution fusion | flops 3019898880 | bytes 13565952 | tf_op jit(solution)/shard_map/dot_general | solution.py:21
  65.4 0.0 copy-start
  65.4 0.0 reduce-scatter.5.cloned.1.call-update
  65.4 0.0 reduce-scatter.9.cloned.1.call-start
  65.5 0.8 copy-done
  66.2 42.1 %all_gather.14 = bf16[640,768]{1,0:T(8,128)(2,1)S(1)} all-gather(bf16[40,768]{1,0:T(8,128)(2,1)S(1)} %copy-done), channel_id=1, replica_groups=mesh['row'=16,'col'=16] {'col'}, dimensions={0}, use_global_device_ids=true | all-gather | bytes 1044480 | tf_op jit(solution)/shard_map/all_gather | solution.py:40
  108.4 7.8 %fusion.9 = f32[640,3072]{1,0:T(8,128)} fusion(bf16[640,768]{1,0:T(8,128)(2,1)S(1)} %all_gather.14, bf16[3072,768]{1,0:T(8,128)(2,1)} %param.6), kind=kOutput, calls=%fused_computation.12 | convolution fusion | flops 3019898880 | bytes 13565952 | tf_op jit(solution)/shard_map/dot_general | solution.py:25
  116.1 0.0 reduce-scatter.9.cloned.1.call-update
  116.2 0.0 all-gather.5.cloned.1.call-start
  116.2 26.5 %reduce-scatter.5.cloned.1.call-done = f32[40,3072]{1,0:T(8,128)} async-done(((f32[640,3072]{1,0:T(8,128)}), f32[40,3072]{1,0:T(8,128)}) %reduce-scatter.5.cloned.1.call-update) | async-done | bytes 491536 | tf_op jit(solution)/shard_map/reduce_scatter | solution.py:32
  142.7 74.7 %reduce-scatter.9.cloned.1.call-done = f32[40,3072]{1,0:T(8,128)} async-done(((f32[640,3072]{1,0:T(8,128)}), f32[40,3072]{1,0:T(8,128)}) %reduce-scatter.9.cloned.1.call-update) | async-done | bytes 491536 | tf_op jit(solution)/shard_map/reduce_scatter | solution.py:41
  217.4 2.3 fusion.6
  219.7 0.0 all-gather.5.cloned.1.call-update
  219.7 0.0 all-gather.3.cloned.1.call-start
  219.8 0.5 all-gather.3.cloned.1.call-update
  220.3 0.0 reduce-scatter.11.cloned.1.call-start
  220.4 41.6 %all-gather.5.cloned.1.call-done = bf16[640,3072]{1,0:T(8,128)(2,1)} async-done(((bf16[40,3072]{1,0:T(8,128)(2,1)}), bf16[640,3072]{1,0:T(8,128)(2,1)}) %all-gather.5.cloned.1.call-update) | async-done | bytes 3932176 | tf_op jit(solution)/shard_map/all_gather | solution.py:45
  262.0 8.1 %fusion.10 = f32[640,768]{1,0:T(8,128)} fusion(bf16[640,3072]{1,0:T(8,128)(2,1)} %all-gather.5.cloned.1.call-done, bf16[768,3072]{1,0:T(8,128)(2,1)} %param.5), kind=kOutput, calls=%fused_computation.13 | convolution fusion | flops 3019898880 | bytes 10616832 | tf_op jit(solution)/shard_map/dot_general | solution.py:25
  270.1 0.0 reduce-scatter.11.cloned.1.call-update
  270.2 0.0 reduce-scatter.7.cloned.1.call-start
  270.2 33.2 %all-gather.3.cloned.1.call-done = bf16[640,3072]{1,0:T(8,128)(2,1)} async-done(((bf16[40,3072]{1,0:T(8,128)(2,1)}), bf16[640,3072]{1,0:T(8,128)(2,1)}) %all-gather.3.cloned.1.call-update) | async-done | bytes 3932176 | tf_op jit(solution)/shard_map/all_gather | solution.py:36
  303.4 8.0 %fusion.8 = f32[640,768]{1,0:T(8,128)} fusion(bf16[640,3072]{1,0:T(8,128)(2,1)} %all-gather.3.cloned.1.call-done, bf16[3072,768]{1,0:T(8,128)(2,1)} %param.6), kind=kOutput, calls=%fused_computation.11 | convolution fusion | flops 3019898880 | bytes 10616832 | tf_op jit(solution)/shard_map/dot_general | solution.py:21
  311.5 0.0 reduce-scatter.7.cloned.1.call-update
  311.5 205.0 %reduce-scatter.11.cloned.1.call-done = f32[40,768]{1,0:T(8,128)} async-done(((f32[640,768]{1,0:T(8,128)}), f32[40,768]{1,0:T(8,128)}) %reduce-scatter.11.cloned.1.call-update) | async-done | bytes 122896 | tf_op jit(solution)/shard_map/reduce_scatter | solution.py:46
  516.5 210.4 %reduce-scatter.7.cloned.1.call-done = f32[40,768]{1,0:T(8,128)} async-done(((f32[640,768]{1,0:T(8,128)}), f32[40,768]{1,0:T(8,128)}) %reduce-scatter.7.cloned.1.call-update) | async-done | bytes 122896 | tf_op jit(solution)/shard_map/reduce_scatter | solution.py:37
Async XLA Ops:
  7.2 135.6 %reduce-scatter.5.cloned.1.call-start = ((), (), s32[]{:S(2)}) async-start(), calls=%async_computation.4 | async-start | bytes 8355840 | tf_op jit(solution)/shard_map/reduce_scatter | solution.py:32
  65.4 0.8 copy-start
  65.4 152.0 %reduce-scatter.9.cloned.1.call-start = ((), (), s32[]{:S(2)}) async-start(), calls=%async_computation.7 | async-start | bytes 8355840 | tf_op jit(solution)/shard_map/reduce_scatter | solution.py:41
  116.2 145.9 %all-gather.5.cloned.1.call-start = ((), (), s32[]{:S(2)}) async-start(), calls=%async_computation.8 | async-start | bytes 4177920 | tf_op jit(solution)/shard_map/all_gather | solution.py:45
  219.7 83.7 %all-gather.3.cloned.1.call-start = ((), (), s32[]{:S(2)}) async-start(), calls=%async_computation.5 | async-start | bytes 4177920 | tf_op jit(solution)/shard_map/all_gather | solution.py:36
  220.3 296.2 %reduce-scatter.11.cloned.1.call-start = ((), (), s32[]{:S(2)}) async-start(), calls=%async_computation.9 | async-start | bytes 2088960 | tf_op jit(solution)/shard_map/reduce_scatter | solution.py:46
  270.2 456.8 %reduce-scatter.7.cloned.1.call-start = ((), (), s32[]{:S(2)}) async-start(), calls=%async_computation.6 | async-start | bytes 2088960 | tf_op jit(solution)/shard_map/reduce_scatter | solution.py:37
Sparse Core Ops, SparseCore 0:
  65.5 77.1 reduce-scatter.4
  145.3 72.1 reduce-scatter.8
  219.9 42.1 all-gather.4
  263.7 39.6 all-gather.2
  307.8 208.6 reduce-scatter.10
  520.8 206.0 reduce-scatter.6
where the time goes:
time: 734 us
  waiting for transfers between devices  592 us (81%)
  blocking collectives  92.6 us (13%)
  matrix products  31.6 us (4%)
  between operations  14.1 us (2%)
    reduce_scatter x1, waiting for transfers between devices, on_device(): lax.psum_scatter(rows_times(activated_full, w_second), 'col', scatter_dim...  210 us
    reduce_scatter x1, waiting for transfers between devices, on_device(): lax.psum_scatter(rows_times_transposed(grad_hidden_full, w_first), 'col',...  205 us
    reduce_scatter x1, waiting for transfers between devices, on_device(): lax.psum_scatter(rows_times_transposed(cotangent_full, w_second), 'row',...  74.7 us
    all_gather x1, blocking collectives, on_device(): input_full = lax.all_gather(inputs, 'col', axis=0, tiled=True)  50.5 us
    all_gather x1, blocking collectives, on_device(): cotangent_full = lax.all_gather(grad_out, 'col', axis=0, tiled=True)  42.1 us
    all_gather x1, waiting for transfers between devices, on_device(): grad_hidden_full = lax.all_gather(grad_hidden, 'row', axis=0, tiled=True)  41.6 us
    all_gather x1, waiting for transfers between devices, on_device(): activated_full = lax.all_gather(activated, 'row', axis=0, tiled=True)  33.2 us
    reduce_scatter x1, waiting for transfers between devices, on_device(): lax.psum_scatter(rows_times(input_full, w_first), 'row', scatter_dimensio...  26.5 us
  transfers between devices with their start and end apart: 6, of which 6 were waited for; matrix products, arithmetic and copies ran while one was open for 3% of the time, Pallas kernels for 0%

commit v1 on v0

v1 whole, which is shorter than its diff:
```python
import functools

import jax
import jax.numpy as jnp
from jax import lax
from jax.experimental import pallas as pl
from jax.experimental.pallas import tpu as pltpu
from jax.sharding import PartitionSpec as P

MESH = pl.DeviceIdType.MESH
F32 = jnp.float32
BF16 = jnp.bfloat16

coef_a = 0.7978845608
coef_b = 0.044715

NY, NZ = 4, 8
LIFT = 2.0**19
DROP = 2.0**-19


def times(panel, weight):
    return jnp.dot(panel, weight, preferred_element_type=F32)


def times_transposed(panel, weight):
    return lax.dot_general(panel, weight, (((1,), (1,)), ((), ())), preferred_element_type=F32)


def coded(v):
    v = v * LIFT
    w = v * v
    w = w * w
    return jnp.where(v < 0, -w, w).astype(BF16)


def decoded(c):
    w = c.astype(F32)
    v = lax.rsqrt(lax.rsqrt(jnp.abs(w))) * DROP
    return jnp.where(w < 0, -v, v)


def kernel(
    T, inp, w1_hbm, w2_hbm, gout, out, gin,
    w1, w2, own, part, unit, sum_f, half_s, half_r, enc1, recv1h, recv1g, enc2h, enc2g, keep2h, keep2g,
    recv2h, recv2g, full, ob, orr, of, ot, mine, xs, xr,
    wsem, part_s, part_r, zp_s, zp_r, zm_s, zm_r, core_s, core_r, r1h_s, r1h_r, r1g_s, r1g_r,
    r2h_s, r2h_r, r2g_s, r2g_r, a1h_s, a1h_r, a1g_s, a1g_r, a2h_s, a2h_r, a2g_s, a2g_r,
    cs_s, cs_r, zo_s, zo_r, xo_s, xo_r,
):
    row = lax.axis_index("row")
    col = lax.axis_index("col")
    xl, y, core = row // 8, (row // 2) % NY, row % 2
    z, xh = col // 2, col % 2
    D = w1.shape[0]
    FF = w1.shape[1]
    HF = FF // 2
    QF = HF // NY
    M = 16 * NZ
    HM = M // 2

    def at_row(a, b, c):
        return (a * 8 + b * 2 + c, col)

    def at_col(a, b):
        return (row, a * 2 + b)

    dev_core = at_row(xl, y, 1 - core)
    dev_x = at_row(1 - xl, y, core)
    dev_y = [at_row(xl, (y + d) % NY, core) for d in range(1, NY)]
    dev_z = [at_col((z + d) % NZ, xh) for d in range(1, NZ)]
    dev_xh = at_col(z, 1 - xh)

    def remote(src, dst, ss, rs, dev):
        return pltpu.make_async_remote_copy(
            src_ref=src, dst_ref=dst, send_sem=ss, recv_sem=rs, device_id=dev, device_id_type=MESH
        )

    my_rows = pl.ds(pl.multiple_of(xl * HM, HM), HM)
    other_rows = pl.ds(pl.multiple_of((1 - xl) * HM, HM), HM)
    base = core * HF
    other_base = (1 - core) * HF

    def cols_of(q):
        return pl.ds(pl.multiple_of(q * QF, 128), QF)

    def full_cols_of(q):
        return pl.ds(pl.multiple_of(base + q * QF, 128), QF)

    my_half = pl.ds(pl.multiple_of(base, 128), HF)
    y_of = [(y + d) % NY for d in range(1, NY)]

    def c_part(k):
        return [remote(own.at[k], part.at[k], part_s.at[k], part_r.at[k], dev_xh)]

    def c_zplus(k, s):
        b = (z - s + NZ) % NZ
        rows = pl.ds(0, 16) if s == 3 else pl.ds(0, 32)
        ref = unit.at[k, b, rows, :]
        return remote(ref, ref, zp_s.at[k, s], zp_r.at[k, s], dev_z[0])

    def c_zminus(k, s):
        b = (z + s) % NZ
        rows = pl.ds(16, 16) if s == 3 else pl.ds(0, 32)
        ref = unit.at[k, b, rows, :]
        return remote(ref, ref, zm_s.at[k, s], zm_r.at[k, s], dev_z[NZ - 2])

    def c_core(k):
        return [remote(half_s.at[k], half_r.at[k], core_s.at[k], core_r.at[k], dev_core)]

    def c_rs1(k):
        got = [remote(enc1.at[k, 0, other_rows, :], recv1h.at[k], r1h_s.at[k], r1h_r.at[k], dev_x)]
        for d in (1, 0, 2):
            got.append(
                remote(
                    enc1.at[k, 1, :, cols_of(y_of[d])], recv1g.at[k, d], r1g_s.at[k, d], r1g_r.at[k, d], dev_y[d]
                )
            )
        return got

    def c_rs2(k):
        got = [remote(enc2g.at[k], recv2g.at[k], r2g_s.at[k], r2g_r.at[k], dev_x)]
        for d in (1, 0, 2):
            got.append(remote(enc2h.at[k, d], recv2h.at[k, d], r2h_s.at[k, d], r2h_r.at[k, d], dev_y[d]))
        return got

    def c_ag1(k):
        ref = full.at[k, 1, my_rows, full_cols_of(y)]
        got = [remote(ref, ref, a1g_s.at[k], a1g_r.at[k], dev_x)]
        ref = full.at[k, 0, my_rows, full_cols_of(y)]
        for d in (1, 0, 2):
            got.append(remote(ref, ref, a1h_s.at[k, d], a1h_r.at[k, d], dev_y[d]))
        return got

    def c_ag2(k):
        ref = full.at[k, 0, my_rows, my_half]
        got = [remote(ref, ref, a2h_s.at[k], a2h_r.at[k], dev_x)]
        ref = full.at[k, 1, :, full_cols_of(y)]
        for d in (1, 0, 2):
            got.append(remote(ref, ref, a2g_s.at[k, d], a2g_r.at[k, d], dev_y[d]))
        return got

    def c_share(k):
        ref = full.at[k, :, :, my_half]
        return [remote(ref, ref, cs_s.at[k], cs_r.at[k], dev_core)]

    def c_zout(k):
        got = []
        for d in (4, 3, 5, 2, 6, 1, 7):
            got.append(
                remote(
                    ob.at[k, (z + d) % NZ], orr.at[k, d - 1], zo_s.at[k, d - 1], zo_r.at[k, d - 1], dev_z[d - 1]
                )
            )
        return got

    def c_xout(k):
        return [remote(xs.at[k], xr.at[k], xo_s.at[k], xo_r.at[k], dev_xh)]

    def start(copies):
        for c in copies:
            c.start()

    def received(copies):
        for c in copies:
            c.wait_recv()

    def sent(copies):
        for c in copies:
            c.wait_send()

    def z_start(k):
        c_zplus(k, 0).start()
        c_zminus(k, 0).start()

    def z_step(k, s):
        c_zplus(k, s - 1).wait_recv()
        c_zplus(k, s).start()
        c_zminus(k, s - 1).wait_recv()
        c_zminus(k, s).start()

    def z_end(k):
        c_zplus(k, 3).wait_recv()
        c_zminus(k, 3).wait_recv()

    def build_unit(k):
        a = own[k].astype(F32)
        b = part[k].astype(F32)

        def joined(v, r):
            return jnp.concatenate([v[r : r + 8], v[r + 8 : r + 16]], axis=1)

        first = xh == 0
        pieces = []
        for r in (0, 16):
            m, o = joined(a, r), joined(b, r)
            pieces += [jnp.where(first, m, o), jnp.where(first, o, m)]
        unit[k, z] = jnp.concatenate(pieces, axis=0).astype(BF16)

    def first_products(k):
        xin = unit[k, :, 0:16, :].reshape(M, D)
        gin_ = unit[k, :, 16:32, :].reshape(M, D)
        step = 512
        for j in range(0, HF, step):
            at = pl.ds(pl.multiple_of(other_base + j, 128), step)
            half_s[k, 0, :, j : j + step] = times(xin, w1[:, at])
        for j in range(0, HF, step):
            at = pl.ds(pl.multiple_of(other_base + j, 128), step)
            half_s[k, 1, :, j : j + step] = times_transposed(gin_, w2[at, :])
        start(c_core(k))
        for j in range(0, HF, step):
            at = pl.ds(pl.multiple_of(base + j, 128), step)
            sum_f[k, 0, :, j : j + step] = times(xin, w1[:, at])
        for j in range(0, HF, step):
            at = pl.ds(pl.multiple_of(base + j, 128), step)
            sum_f[k, 1, :, j : j + step] = times_transposed(gin_, w2[at, :])

    def reduce_first(k):
        received(c_core(k))
        enc1[k, 0, other_rows, :] = coded(sum_f[k, 0, other_rows, :] + half_r[k, 0, other_rows, :])
        for d in range(NY - 1):
            at = cols_of(y_of[d])
            enc1[k, 1, :, at] = coded(sum_f[k, 1, :, at] + half_r[k, 1, :, at])
        start(c_rs1(k))
        sum_f[k, 0, my_rows, :] = sum_f[k, 0, my_rows, :] + half_r[k, 0, my_rows, :]
        at = cols_of(y)
        sum_f[k, 1, :, at] = sum_f[k, 1, :, at] + half_r[k, 1, :, at]

    def reduce_second(k):
        received(c_rs1(k))
        for d in range(NY - 1):
            at = cols_of(y_of[d])
            enc2h[k, d] = coded(sum_f[k, 0, my_rows, at] + decoded(recv1h[k, :, at]))
        at = cols_of(y)

        def total(rows):
            got = sum_f[k, 1, rows, at]
            for d in range(NY - 1):
                got = got + decoded(recv1g[k, d, rows, :])
            return got

        enc2g[k] = coded(total(other_rows))
        start(c_rs2(k))
        keep2h[k] = sum_f[k, 0, my_rows, at] + decoded(recv1h[k, :, at])
        keep2g[k] = total(my_rows)

    def activate(k):
        received(c_rs2(k))
        h = keep2h[k]
        for d in range(NY - 1):
            h = h + decoded(recv2h[k, d])
        g = keep2g[k] + decoded(recv2g[k])
        t = jnp.tanh(coef_a * (h + coef_b * h * h * h))
        act = 0.5 * h * (1.0 + t)
        slope = 0.5 * (1.0 + t) + 0.5 * h * (1.0 - t * t) * coef_a * (1.0 + 3.0 * coef_b * h * h)
        full[k, 0, my_rows, full_cols_of(y)] = act.astype(BF16)
        full[k, 1, my_rows, full_cols_of(y)] = (g * slope).astype(BF16)
        start(c_ag1(k))

    def gather_second(k):
        received(c_ag1(k))
        start(c_ag2(k))

    def gather_third(k):
        received(c_ag2(k))
        start(c_share(k))

    def second_products(k):
        received(c_share(k))
        o = times(full[k, 0], w2[...]).reshape(NZ, 16, D)
        ot[0] = o
        ob[k, :, 0:16, :] = o.astype(BF16)
        o = times_transposed(full[k, 1], w1[...]).reshape(NZ, 16, D)
        ot[1] = o
        ob[k, :, 16:32, :] = o.astype(BF16)
        start(c_zout(k))
        of[k] = ot[:, z]

    def reduce_out(k):
        received(c_zout(k))
        total = of[k].reshape(32, D)
        for d in range(NZ - 1):
            total = total + orr[k, d].astype(F32)
        first = xh == 0
        for i in range(2):
            lo, hi = total[16 * i : 16 * i + 8], total[16 * i + 8 : 16 * i + 16]
            mine[k, 8 * i : 8 * i + 8, :] = jnp.where(first, lo, hi)
            xs[k, 8 * i : 8 * i + 8, :] = jnp.where(first, hi, lo)
        start(c_xout(k))

    def finish(k):
        received(c_xout(k))
        at = pl.ds(pl.multiple_of(8 * k, 8), 8)
        out[at, :] = mine[k, 0:8, :] + xr[k, 0:8, :]
        gin[at, :] = mine[k, 8:16, :] + xr[k, 8:16, :]

    cw1 = pltpu.make_async_copy(w1_hbm, w1, wsem.at[0])
    cw2 = pltpu.make_async_copy(w2_hbm, w2, wsem.at[1])
    cw1.start()
    cw2.start()
    peers = [dev_core, dev_x, dev_xh] + dev_y + dev_z
    barrier = pltpu.get_barrier_semaphore()
    for p in peers:
        pl.semaphore_signal(barrier, inc=1, device_id=p, device_id_type=MESH)
    a = inp[...].astype(F32)
    g = gout[...].astype(F32)
    hd = D // 2
    for k in range(T):
        s = slice(8 * k, 8 * k + 8)
        own[k] = jnp.concatenate([a[s, :hd], a[s, hd:], g[s, :hd], g[s, hd:]], axis=0).astype(BF16)
    pl.semaphore_wait(barrier, len(peers))
    for k in range(T):
        start(c_part(k))
    received(c_part(0))
    build_unit(0)
    z_start(0)
    for s in range(1, T):
        received(c_part(s))
        build_unit(s)
    for s in range(1, 4):
        z_step(0, s)
    cw1.wait()
    cw2.wait()
    z_end(0)
    first_products(0)

    def step(t, carry):
        def when(k, body):
            @pl.when(jnp.logical_and(k >= 0, k < T))
            def _():
                body(k)

        when(t - 1, activate)
        when(t, reduce_first)
        when(t + 1, z_start)
        when(t - 2, gather_third)
        when(t + 1, lambda k: z_step(k, 1))
        when(t - 3, reduce_out)
        when(t - 2, second_products)
        when(t + 1, lambda k: z_step(k, 2))
        when(t - 1, gather_second)
        when(t, reduce_second)
        when(t + 1, lambda k: z_step(k, 3))
        when(t + 1, z_end)
        when(t + 1, first_products)
        when(t - 3, finish)
        return carry

    lax.fori_loop(0, T + 3, step, 0)

    def drain(k, carry):
        for copies in (c_part, c_core, c_rs1, c_rs2, c_ag1, c_ag2, c_share, c_zout, c_xout):
            sent(copies(k))
        for s in range(4):
            c_zplus(k, s).wait_send()
            c_zminus(k, s).wait_send()
        return carry

    lax.fori_loop(0, T, drain, 0)


def on_device(inputs, w_first, w_second, grad_out):
    tokens, D = inputs.shape
    FF = w_first.shape[1]
    T = tokens // 8
    M = 16 * NZ
    HM, HF = M // 2, FF // 2
    QF = HF // NY
    V = pl.BlockSpec(memory_space=pltpu.VMEM)
    ANY = pl.BlockSpec(memory_space=pl.ANY)
    shape = jax.ShapeDtypeStruct((tokens, D), F32)
    dma = pltpu.SemaphoreType.DMA
    one, three = dma((T,)), dma((T, NY - 1))
    buffers = [
        pltpu.VMEM((D, FF), BF16),
        pltpu.VMEM((FF, D), BF16),
        pltpu.VMEM((T, 32, D // 2), BF16),
        pltpu.VMEM((T, 32, D // 2), BF16),
        pltpu.VMEM((T, NZ, 32, D), BF16),
        pltpu.VMEM((T, 2, M, HF), F32),
        pltpu.VMEM((T, 2, M, HF), F32),
        pltpu.VMEM((T, 2, M, HF), F32),
        pltpu.VMEM((T, 2, M, HF), BF16),
        pltpu.VMEM((T, HM, HF), BF16),
        pltpu.VMEM((T, NY - 1, M, QF), BF16),
        pltpu.VMEM((T, NY - 1, HM, QF), BF16),
        pltpu.VMEM((T, HM, QF), BF16),
        pltpu.VMEM((T, HM, QF), F32),
        pltpu.VMEM((T, HM, QF), F32),
        pltpu.VMEM((T, NY - 1, HM, QF), BF16),
        pltpu.VMEM((T, HM, QF), BF16),
        pltpu.VMEM((T, 2, M, FF), BF16),
        pltpu.VMEM((T, NZ, 32, D), BF16),
        pltpu.VMEM((T, NZ - 1, 32, D), BF16),
        pltpu.VMEM((T, 2, 16, D), F32),
        pltpu.VMEM((2, NZ, 16, D), F32),
        pltpu.VMEM((T, 16, D), F32),
        pltpu.VMEM((T, 16, D), F32),
        pltpu.VMEM((T, 16, D), F32),
    ]
    semaphores = [
        dma((2,)),
        one, one,
        dma((T, 4)), dma((T, 4)), dma((T, 4)), dma((T, 4)),
        one, one,
        one, one, three, three,
        three, three, one, one,
        three, three, one, one,
        one, one, three, three,
        one, one,
        dma((T, NZ - 1)), dma((T, NZ - 1)),
        one, one,
    ]
    flops = 4 * 2 * M * T * D * FF
    return pl.pallas_call(
        functools.partial(kernel, T),
        out_shape=(shape, shape),
        in_specs=[V, ANY, ANY, V],
        out_specs=(V, V),
        scratch_shapes=buffers + semaphores,
        compiler_params=pltpu.CompilerParams(
            collective_id=0, has_side_effects=True, vmem_limit_bytes=63 * 2**20
        ),
        cost_estimate=pl.CostEstimate(flops=flops, bytes_accessed=4 * D * FF, transcendentals=0),
    )(inputs, w_first, w_second, grad_out)


def solution(mesh):
    in_specs = (P("col", "row"), P("row", "col"), P("col", "row"), P("col", "row"))
    out_specs = (P("col", "row"), P("col", "row"))
    return jax.shard_map(
        on_device, mesh=mesh, in_specs=in_specs, out_specs=out_specs, check_vma=False
    )
```

time: 734 us -> 170 us (0.23)
  waiting for transfers between devices: 592 us -> 0 us
  Pallas kernels: 0 us -> 164 us
  blocking collectives: 92.6 us -> 0 us
  matrix products: 31.6 us -> 0 us
  between operations: 14.1 us -> 0.64 us
    reduce_scatter x4 -> x0, waiting for transfers between devices: 517 us -> none  [the longest x1 210 us: on_device(): lax.psum_scatter(rows_times(activated_full, w_second), 'col', scatter_dim...]
    pallas_call x0 -> x1, Pallas kernels: none -> 164 us  [on_device(): pl.pallas_call(functools.partial(kernel, T), out_shape=(shape, shape), in...]
    all_gather x2 -> x0, blocking collectives: 92.6 us -> none  [the longest x1 50.5 us: on_device(): input_full = lax.all_gather(inputs, 'col', axis=0, tiled=True)]
    all_gather x2 -> x0, waiting for transfers between devices: 74.9 us -> none  [the longest x1 41.6 us: on_device(): grad_hidden_full = lax.all_gather(grad_hidden, 'row', axis=0, tiled=True)]
    dot_general x4 -> x0, matrix products: 31.6 us -> none  [the longest x2 15.9 us: rows_times_transposed(): lax.dot_general(panel, weight, (((1,), (1,)), ((), ())), preferred_elemen...]
  transfers between devices with their start and end apart: 6 -> 0, of which waited for: 6 -> 0; matrix products, arithmetic and copies ran while one was open for 3% -> 0% of each run, Pallas kernels for 0% -> 0%
where the time goes in v1:
time: 170 us; the launch traced here: 168 us
  Pallas kernels  164 us (96%)
  local copies, waits for them, and re-layouts  3.12 us (2%)
    pallas_call x1, Pallas kernels, on_device(): pl.pallas_call(functools.partial(kernel, T), out_shape=(shape, shape), in...  164 us

profile of v1, /device:TPU:8, one launch (start us, length us, event | category | flops | bytes accessed | tf_op | source)
XLA Modules:
  0.0 168.1 jit_solution(11900664595827496998)
XLA Ops:
  0.6 164.3 %shard_map.59 = (f32[40,768]{1,0:T(8,128)}, f32[40,768]{1,0:T(8,128)}) custom-call(bf16[40,768]{1,0:T(8,128)(2,1)} %inp.1, bf16[768,3072]{1,0:T(8,128)(2,1)} %w1_hbm.1, bf16[3072,768]{1,0:T(8,128)(2,1)} %w2_hbm.1, bf16[40,768]{1,0:T(8,128)(2,1)} %gout.1), custom_call_target="tpu_custom_call" | custom-call | flops 12079595520 | bytes 9437184 | tf_op jit(solution)/shard_map/pallas_call | solution.py:415
  165.0 1.6 copy.8
  166.5 1.6 copy.9

commit v2 on v1

--- a/solution.py
+++ b/solution.py
@@ -15,8 +15,9 @@
 coef_b = 0.044715
 
 NY, NZ = 4, 8
+NEAR = (3, 5, 2, 6, 1, 7)
 LIFT = 2.0**19
-DROP = 2.0**-19
+LIFT_OUT = 2.0**8
 
 
 def times(panel, weight):
@@ -27,26 +28,26 @@
     return lax.dot_general(panel, weight, (((1,), (1,)), ((), ())), preferred_element_type=F32)
 
 
-def coded(v):
-    v = v * LIFT
+def coded(v, lift=LIFT):
+    v = v * lift
     w = v * v
     w = w * w
     return jnp.where(v < 0, -w, w).astype(BF16)
 
 
-def decoded(c):
+def decoded(c, lift=LIFT):
     w = c.astype(F32)
-    v = lax.rsqrt(lax.rsqrt(jnp.abs(w))) * DROP
+    v = lax.rsqrt(lax.rsqrt(jnp.abs(w))) * (1.0 / lift)
     return jnp.where(w < 0, -v, v)
 
 
 def kernel(
     T, inp, w1_hbm, w2_hbm, gout, out, gin,
     w1, w2, own, part, unit, sum_f, half_s, half_r, enc1, recv1h, recv1g, enc2h, enc2g, keep2h, keep2g,
-    recv2h, recv2g, full, ob, orr, of, ot, mine, xs, xr,
-    wsem, part_s, part_r, zp_s, zp_r, zm_s, zm_r, core_s, core_r, r1h_s, r1h_r, r1g_s, r1g_r,
+    recv2h, recv2g, full, out_s, out_r, far_s, far_r, ot, mine, xs, xr,
+    wsem, part_s, part_r, zn_s, zn_r, zf_s, zf_r, core_s, core_r, r1h_s, r1h_r, r1g_s, r1g_r,
     r2h_s, r2h_r, r2g_s, r2g_r, a1h_s, a1h_r, a1g_s, a1g_r, a2h_s, a2h_r, a2g_s, a2g_r,
-    cs_s, cs_r, zo_s, zo_r, xo_s, xo_r,
+    cs_s, cs_r, on_s, on_r, of_s, of_r, xo_s, xo_r,
 ):
     row = lax.axis_index("row")
     col = lax.axis_index("col")
@@ -68,7 +69,7 @@
     dev_core = at_row(xl, y, 1 - core)
     dev_x = at_row(1 - xl, y, core)
     dev_y = [at_row(xl, (y + d) % NY, core) for d in range(1, NY)]
-    dev_z = [at_col((z + d) % NZ, xh) for d in range(1, NZ)]
+    dev_z = [at_col((z + d) % NZ, xh) for d in range(NZ)]
     dev_xh = at_col(z, 1 - xh)
 
     def remote(src, dst, ss, rs, dev):
@@ -93,17 +94,16 @@
     def c_part(k):
         return [remote(own.at[k], part.at[k], part_s.at[k], part_r.at[k], dev_xh)]
 
-    def c_zplus(k, s):
-        b = (z - s + NZ) % NZ
-        rows = pl.ds(0, 16) if s == 3 else pl.ds(0, 32)
-        ref = unit.at[k, b, rows, :]
-        return remote(ref, ref, zp_s.at[k, s], zp_r.at[k, s], dev_z[0])
-
-    def c_zminus(k, s):
-        b = (z + s) % NZ
-        rows = pl.ds(16, 16) if s == 3 else pl.ds(0, 32)
-        ref = unit.at[k, b, rows, :]
-        return remote(ref, ref, zm_s.at[k, s], zm_r.at[k, s], dev_z[NZ - 2])
+    def c_near(k, ds=NEAR):
+        ref = unit.at[k, z]
+        return [remote(ref, ref, zn_s.at[k, d - 1], zn_r.at[k, d - 1], dev_z[d]) for d in ds]
+
+    def c_far(k):
+        got = []
+        for i, (b, d) in enumerate(((NZ - 3, 1), (3, NZ - 1))):
+            ref = unit.at[k, (z + b) % NZ, pl.ds(16 * i, 16), :]
+            got.append(remote(ref, ref, zf_s.at[k, i], zf_r.at[k, i], dev_z[d]))
+        return got
 
     def c_core(k):
         return [remote(half_s.at[k], half_r.at[k], core_s.at[k], core_r.at[k], dev_core)]
@@ -144,13 +144,17 @@
         ref = full.at[k, :, :, my_half]
         return [remote(ref, ref, cs_s.at[k], cs_r.at[k], dev_core)]
 
-    def c_zout(k):
+    def c_out(k, ds):
+        return [
+            remote(out_s.at[k, d - 1], out_r.at[k, d - 1], on_s.at[k, d - 1], on_r.at[k, d - 1], dev_z[d]) for d in ds
+        ]
+
+    def c_out_far(k):
         got = []
-        for d in (4, 3, 5, 2, 6, 1, 7):
+        for i, d in enumerate((1, NZ - 1)):
+            rows = pl.ds(16 * i, 16)
             got.append(
-                remote(
-                    ob.at[k, (z + d) % NZ], orr.at[k, d - 1], zo_s.at[k, d - 1], zo_r.at[k, d - 1], dev_z[d - 1]
-                )
+                remote(far_s.at[k, rows, :], far_r.at[k, rows, :], of_s.at[k, i], of_r.at[k, i], dev_z[d])
             )
         return got
 
@@ -170,18 +174,15 @@
             c.wait_send()
 
     def z_start(k):
-        c_zplus(k, 0).start()
-        c_zminus(k, 0).start()
-
-    def z_step(k, s):
-        c_zplus(k, s - 1).wait_recv()
-        c_zplus(k, s).start()
-        c_zminus(k, s - 1).wait_recv()
-        c_zminus(k, s).start()
+        start(c_near(k))
+
+    def z_pass(k):
+        received(c_near(k, NEAR[:2]))
+        start(c_far(k))
 
     def z_end(k):
-        c_zplus(k, 3).wait_recv()
-        c_zminus(k, 3).wait_recv()
+        received(c_near(k, NEAR[2:]))
+        received(c_far(k))
 
     def build_unit(k):
         a = own[k].astype(F32)
@@ -265,22 +266,41 @@
         received(c_ag2(k))
         start(c_share(k))
 
+    def own_out(k, b):
+        return ot[k % 3, :, b].reshape(32, D)
+
+    def out_first(k):
+        v = own_out(k, (z + 4) % NZ)
+        far_s[k] = coded(v, LIFT_OUT)
+        start(c_out_far(k))
+        for d in (2, 6, 1, 7):
+            out_s[k, d - 1] = coded(own_out(k, (z + d) % NZ), LIFT_OUT)
+            start(c_out(k, (d,)))
+
+    def out_second(k):
+        c = c_out_far(k)
+        c[0].wait_recv()
+        v = own_out(k, (z + 3) % NZ)
+        out_s[k, 2, 0:16, :] = coded(v[0:16] + decoded(far_r[k, 0:16, :], LIFT_OUT), LIFT_OUT)
+        out_s[k, 2, 16:32, :] = coded(v[16:32], LIFT_OUT)
+        start(c_out(k, (3,)))
+        c[1].wait_recv()
+        v = own_out(k, (z + 5) % NZ)
+        out_s[k, 4, 0:16, :] = coded(v[0:16], LIFT_OUT)
+        out_s[k, 4, 16:32, :] = coded(v[16:32] + decoded(far_r[k, 16:32, :], LIFT_OUT), LIFT_OUT)
+        start(c_out(k, (5,)))
+
     def second_products(k):
         received(c_share(k))
-        o = times(full[k, 0], w2[...]).reshape(NZ, 16, D)
-        ot[0] = o
-        ob[k, :, 0:16, :] = o.astype(BF16)
-        o = times_transposed(full[k, 1], w1[...]).reshape(NZ, 16, D)
-        ot[1] = o
-        ob[k, :, 16:32, :] = o.astype(BF16)
-        start(c_zout(k))
-        of[k] = ot[:, z]
+        ot[k % 3, 0] = times(full[k, 0], w2[...]).reshape(NZ, 16, D)
+        ot[k % 3, 1] = times_transposed(full[k, 1], w1[...]).reshape(NZ, 16, D)
+        out_first(k)
 
     def reduce_out(k):
-        received(c_zout(k))
-        total = of[k].reshape(32, D)
-        for d in range(NZ - 1):
-            total = total + orr[k, d].astype(F32)
+        received(c_out(k, NEAR))
+        total = own_out(k, z)
+        for d in NEAR:
+            total = total + decoded(out_r[k, d - 1], LIFT_OUT)
         first = xh == 0
         for i in range(2):
             lo, hi = total[16 * i : 16 * i + 8], total[16 * i + 8 : 16 * i + 16]
@@ -298,7 +318,7 @@
     cw2 = pltpu.make_async_copy(w2_hbm, w2, wsem.at[1])
     cw1.start()
     cw2.start()
-    peers = [dev_core, dev_x, dev_xh] + dev_y + dev_z
+    peers = [dev_core, dev_x, dev_xh] + dev_y + [dev_z[d] for d in NEAR]
     barrier = pltpu.get_barrier_semaphore()
     for p in peers:
         pl.semaphore_signal(barrier, inc=1, device_id=p, device_id_type=MESH)
@@ -314,15 +334,13 @@
     received(c_part(0))
     build_unit(0)
     z_start(0)
-    for s in range(1, T):
-        received(c_part(s))
-        build_unit(s)
-    for s in range(1, 4):
-        z_step(0, s)
+    for k in range(1, T):
+        received(c_part(k))
+        build_unit(k)
+    z_pass(0)
+    z_start(1)
     cw1.wait()
     cw2.wait()
-    z_end(0)
-    first_products(0)
 
     def step(t, carry):
         def when(k, body):
@@ -331,32 +349,50 @@
                 body(k)
 
         when(t - 1, activate)
-        when(t, reduce_first)
-        when(t + 1, z_start)
-        when(t - 2, gather_third)
-        when(t + 1, lambda k: z_step(k, 1))
-        when(t - 3, reduce_out)
-        when(t - 2, second_products)
-        when(t + 1, lambda k: z_step(k, 2))
-        when(t - 1, gather_second)
         when(t, reduce_second)
-        when(t + 1, lambda k: z_step(k, 3))
-        when(t + 1, z_end)
-        when(t + 1, first_products)
-        when(t - 3, finish)
+        when(t - 2, gather_second)
+        when(t - 4, out_second)
+        when(t + 1, reduce_first)
+        when(t - 3, gather_third)
+        when(t + 2, z_end)
+        when(t + 2, first_products)
+        when(t - 5, finish)
+        when(t - 3, second_products)
+        when(t - 4, reduce_out)
+
+        @pl.when(jnp.logical_and(t + 3 >= 1, t + 3 < T))
+        def _():
+            z_pass(t + 3)
+
+        @pl.when(jnp.logical_and(t + 4 >= 2, t + 4 < T))
+        def _():
+            z_start(t + 4)
+
         return carry
 
-    lax.fori_loop(0, T + 3, step, 0)
+    lax.fori_loop(-2, T + 3, step, 0)
 
     def drain(k, carry):
-        for copies in (c_part, c_core, c_rs1, c_rs2, c_ag1, c_ag2, c_share, c_zout, c_xout):
+        for copies in (c_part, c_core, c_rs1, c_rs2, c_ag1, c_ag2, c_share):
             sent(copies(k))
-        for s in range(4):
-            c_zplus(k, s).wait_send()
-            c_zminus(k, s).wait_send()
+        sent(c_near(k))
+        sent(c_far(k))
         return carry
 
+    def drain_out(k, carry):
+        sent(c_out_far(k))
+        sent(c_out(k, NEAR))
+        sent(c_xout(k))
+        return carry
+
+    last = T - 1
+    out_second(last)
+    finish(last - 1)
     lax.fori_loop(0, T, drain, 0)
+    lax.fori_loop(0, last, drain_out, 0)
+    reduce_out(last)
+    finish(last)
+    drain_out(last, 0)
 
 
 def on_device(inputs, w_first, w_second, grad_out):
@@ -390,10 +426,11 @@
         pltpu.VMEM((T, NY - 1, HM, QF), BF16),
         pltpu.VMEM((T, HM, QF), BF16),
         pltpu.VMEM((T, 2, M, FF), BF16),
-        pltpu.VMEM((T, NZ, 32, D), BF16),
         pltpu.VMEM((T, NZ - 1, 32, D), BF16),
-        pltpu.VMEM((T, 2, 16, D), F32),
-        pltpu.VMEM((2, NZ, 16, D), F32),
+        pltpu.VMEM((T, NZ - 1, 32, D), BF16),
+        pltpu.VMEM((T, 32, D), BF16),
+        pltpu.VMEM((T, 32, D), BF16),
+        pltpu.VMEM((3, 2, NZ, 16, D), F32),
         pltpu.VMEM((T, 16, D), F32),
         pltpu.VMEM((T, 16, D), F32),
         pltpu.VMEM((T, 16, D), F32),
@@ -401,14 +438,14 @@
     semaphores = [
         dma((2,)),
         one, one,
-        dma((T, 4)), dma((T, 4)), dma((T, 4)), dma((T, 4)),
+        dma((T, NZ - 1)), dma((T, NZ - 1)), dma((T, 2)), dma((T, 2)),
         one, one,
         one, one, three, three,
         three, three, one, one,
         three, three, one, one,
         one, one, three, three,
         one, one,
-        dma((T, NZ - 1)), dma((T, NZ - 1)),
+        dma((T, NZ - 1)), dma((T, NZ - 1)), dma((T, 2)), dma((T, 2)),
         one, one,
     ]
     flops = 4 * 2 * M * T * D * FF

time: 170 us -> 131 us (0.77)
  Pallas kernels: 164 us -> 125 us
    pallas_call x1, Pallas kernels: 164 us -> 125 us  [on_device(): pl.pallas_call(functools.partial(kernel, T), out_shape=(shape, shape), in...]
where the time goes in v2:
time: 131 us; the launch traced here: 129 us
  Pallas kernels  125 us (95%)
  local copies, waits for them, and re-layouts  3.12 us (2%)
    pallas_call x1, Pallas kernels, on_device(): pl.pallas_call(functools.partial(kernel, T), out_shape=(shape, shape), in...  125 us
    unnamed x2, local copies, waits for them, and re-layouts  3.12 us

profile of v2, /device:TPU:8, one launch (start us, length us, event | category | flops | bytes accessed | tf_op | source)
XLA Modules:
  0.0 128.9 jit_solution(12870033723494253167)
XLA Ops:
  0.6 125.1 %shard_map.59 = (f32[40,768]{1,0:T(8,128)}, f32[40,768]{1,0:T(8,128)}) custom-call(bf16[40,768]{1,0:T(8,128)(2,1)} %inp.1, bf16[768,3072]{1,0:T(8,128)(2,1)} %w1_hbm.1, bf16[3072,768]{1,0:T(8,128)(2,1)} %w2_hbm.1, bf16[40,768]{1,0:T(8,128)(2,1)} %gout.1), custom_call_target="tpu_custom_call" | custom-call | flops 12079595520 | bytes 9437184 | tf_op jit(solution)/shard_map/pallas_call | solution.py:452
  125.8 1.6 %copy.8 = f32[40,768]{1,0:T(8,128)} copy(f32[40,768]{1,0:T(8,128)} %get-tuple-element.4) | data formatting | bytes 245760
  127.3 1.6 %copy.9 = f32[40,768]{1,0:T(8,128)} copy(f32[40,768]{1,0:T(8,128)} %get-tuple-element.5) | data formatting | bytes 245760

commit v3 on v2

--- a/solution.py
+++ b/solution.py
@@ -204,10 +204,10 @@
         step = 512
         for j in range(0, HF, step):
             at = pl.ds(pl.multiple_of(other_base + j, 128), step)
-            half_s[k, 0, :, j : j + step] = times(xin, w1[:, at])
+            half_s[k, 0, :, j : j + step] = coded(times(xin, w1[:, at]))
         for j in range(0, HF, step):
             at = pl.ds(pl.multiple_of(other_base + j, 128), step)
-            half_s[k, 1, :, j : j + step] = times_transposed(gin_, w2[at, :])
+            half_s[k, 1, :, j : j + step] = coded(times_transposed(gin_, w2[at, :]))
         start(c_core(k))
         for j in range(0, HF, step):
             at = pl.ds(pl.multiple_of(base + j, 128), step)
@@ -218,14 +218,14 @@
 
     def reduce_first(k):
         received(c_core(k))
-        enc1[k, 0, other_rows, :] = coded(sum_f[k, 0, other_rows, :] + half_r[k, 0, other_rows, :])
+        enc1[k, 0, other_rows, :] = coded(sum_f[k, 0, other_rows, :] + decoded(half_r[k, 0, other_rows, :]))
         for d in range(NY - 1):
             at = cols_of(y_of[d])
-            enc1[k, 1, :, at] = coded(sum_f[k, 1, :, at] + half_r[k, 1, :, at])
+            enc1[k, 1, :, at] = coded(sum_f[k, 1, :, at] + decoded(half_r[k, 1, :, at]))
         start(c_rs1(k))
-        sum_f[k, 0, my_rows, :] = sum_f[k, 0, my_rows, :] + half_r[k, 0, my_rows, :]
+        sum_f[k, 0, my_rows, :] = sum_f[k, 0, my_rows, :] + decoded(half_r[k, 0, my_rows, :])
         at = cols_of(y)
-        sum_f[k, 1, :, at] = sum_f[k, 1, :, at] + half_r[k, 1, :, at]
+        sum_f[k, 1, :, at] = sum_f[k, 1, :, at] + decoded(half_r[k, 1, :, at])
 
     def reduce_second(k):
         received(c_rs1(k))
@@ -279,12 +279,12 @@
 
     def out_second(k):
         c = c_out_far(k)
-        c[0].wait_recv()
+        received(c[:1])
         v = own_out(k, (z + 3) % NZ)
         out_s[k, 2, 0:16, :] = coded(v[0:16] + decoded(far_r[k, 0:16, :], LIFT_OUT), LIFT_OUT)
         out_s[k, 2, 16:32, :] = coded(v[16:32], LIFT_OUT)
         start(c_out(k, (3,)))
-        c[1].wait_recv()
+        received(c[1:])
         v = own_out(k, (z + 5) % NZ)
         out_s[k, 4, 0:16, :] = coded(v[0:16], LIFT_OUT)
         out_s[k, 4, 16:32, :] = coded(v[16:32] + decoded(far_r[k, 16:32, :], LIFT_OUT), LIFT_OUT)
@@ -351,9 +351,9 @@
         when(t - 1, activate)
         when(t, reduce_second)
         when(t - 2, gather_second)
-        when(t - 4, out_second)
         when(t + 1, reduce_first)
         when(t - 3, gather_third)
+        when(t - 4, out_second)
         when(t + 2, z_end)
         when(t + 2, first_products)
         when(t - 5, finish)
@@ -393,6 +393,11 @@
     reduce_out(last)
     finish(last)
     drain_out(last, 0)
+
+
+def hand_over(a, b, out, gin):
+    out[...] = a[...]
+    gin[...] = b[...]
 
 
 def on_device(inputs, w_first, w_second, grad_out):
@@ -414,8 +419,8 @@
         pltpu.VMEM((T, 32, D // 2), BF16),
         pltpu.VMEM((T, NZ, 32, D), BF16),
         pltpu.VMEM((T, 2, M, HF), F32),
-        pltpu.VMEM((T, 2, M, HF), F32),
-        pltpu.VMEM((T, 2, M, HF), F32),
+        pltpu.VMEM((T, 2, M, HF), BF16),
+        pltpu.VMEM((T, 2, M, HF), BF16),
         pltpu.VMEM((T, 2, M, HF), BF16),
         pltpu.VMEM((T, HM, HF), BF16),
         pltpu.VMEM((T, NY - 1, M, QF), BF16),
@@ -449,7 +454,7 @@
         one, one,
     ]
     flops = 4 * 2 * M * T * D * FF
-    return pl.pallas_call(
+    parts = pl.pallas_call(
         functools.partial(kernel, T),
         out_shape=(shape, shape),
         in_specs=[V, ANY, ANY, V],
@@ -460,6 +465,7 @@
         ),
         cost_estimate=pl.CostEstimate(flops=flops, bytes_accessed=4 * D * FF, transcendentals=0),
     )(inputs, w_first, w_second, grad_out)
+    return pl.pallas_call(hand_over, out_shape=(shape, shape), in_specs=[V, V], out_specs=(V, V))(*parts)
 
 
 def solution(mesh):

time: 131 us -> 128 us (0.977)
  local copies, waits for them, and re-layouts: 3.12 us -> 0 us
    unnamed x2 -> x0, local copies, waits for them, and re-layouts: 3.12 us -> none
    pallas_call x0 -> x1, Pallas kernels: none -> 1.66 us  [on_device(): pl.pallas_call(hand_over, out_shape=(shape, shape), in_specs=[V, V], out_...]
    pallas_call x1, Pallas kernels: 125 us -> 124 us  [on_device(): pl.pallas_call(functools.partial(kernel, T), out_shape=(shape, shape), in...]
where the time goes in v3:
time: 128 us; the launch traced here: 126 us
  Pallas kernels  125 us (98%)
    pallas_call x1, Pallas kernels, on_device(): pl.pallas_call(functools.partial(kernel, T), out_shape=(shape, shape), in...  124 us

profile of v3, /device:TPU:8, one launch (start us, length us, event | category | flops | bytes accessed | tf_op | source)
XLA Modules:
  0.0 126.0 jit_solution(3090317871545211179)
XLA Ops:
  0.6 123.7 %shard_map.59 = (f32[40,768]{1,0:T(8,128)}, f32[40,768]{1,0:T(8,128)}) custom-call(bf16[40,768]{1,0:T(8,128)(2,1)} %inp.1, bf16[768,3072]{1,0:T(8,128)(2,1)} %w1_hbm.1, bf16[3072,768]{1,0:T(8,128)(2,1)} %w2_hbm.1, bf16[40,768]{1,0:T(8,128)(2,1)} %gout.1), custom_call_target="tpu_custom_call" | custom-call | flops 12079595520 | bytes 9437184 | tf_op jit(solution)/shard_map/pallas_call | solution.py:457
  124.4 1.7 %shard_map.60 = (f32[40,768]{1,0:T(8,128)}, f32[40,768]{1,0:T(8,128)}) custom-call(f32[40,768]{1,0:T(8,128)} %get-tuple-element.4.a, f32[40,768]{1,0:T(8,128)} %get-tuple-element.5.b), custom_call_target="tpu_custom_call" | custom-call | tf_op jit(solution)/shard_map/pallas_call | solution.py:468

commit v4 on v3

--- a/solution.py
+++ b/solution.py
@@ -141,8 +141,8 @@
         return got
 
     def c_share(k):
-        ref = full.at[k, :, :, my_half]
-        return [remote(ref, ref, cs_s.at[k], cs_r.at[k], dev_core)]
+        refs = [full.at[k, i, :, my_half] for i in range(2)]
+        return [remote(r, r, cs_s.at[k, i], cs_r.at[k, i], dev_core) for i, r in enumerate(refs)]
 
     def c_out(k, ds):
         return [
@@ -291,8 +291,10 @@
         start(c_out(k, (5,)))
 
     def second_products(k):
-        received(c_share(k))
+        share = c_share(k)
+        received(share[:1])
         ot[k % 3, 0] = times(full[k, 0], w2[...]).reshape(NZ, 16, D)
+        received(share[1:])
         ot[k % 3, 1] = times_transposed(full[k, 1], w1[...]).reshape(NZ, 16, D)
         out_first(k)
 
@@ -449,7 +451,7 @@
         three, three, one, one,
         three, three, one, one,
         one, one, three, three,
-        one, one,
+        dma((T, 2)), dma((T, 2)),
         dma((T, NZ - 1)), dma((T, NZ - 1)), dma((T, 2)), dma((T, 2)),
         one, one,
     ]

time: 128 us -> 128 us (level); the launches traced: 126 us -> 127 us
  Pallas kernels: 125 us -> 127 us
    pallas_call x1, Pallas kernels: 124 us -> 125 us  [on_device(): pl.pallas_call(functools.partial(kernel, T), out_shape=(shape, shape), in...]
where the time goes in v4:
time: 128 us; the launch traced here: 127 us
  Pallas kernels  127 us (99%)
    pallas_call x1, Pallas kernels, on_device(): pl.pallas_call(functools.partial(kernel, T), out_shape=(shape, shape), in...  125 us

profile of v4, /device:TPU:8, one launch (start us, length us, event | category | flops | bytes accessed | tf_op | source)
XLA Modules:
  0.0 127.5 jit_solution(4624778303708285704)
XLA Ops:
  0.6 125.2 %shard_map.59 = (f32[40,768]{1,0:T(8,128)}, f32[40,768]{1,0:T(8,128)}) custom-call(bf16[40,768]{1,0:T(8,128)(2,1)} %inp.1, bf16[768,3072]{1,0:T(8,128)(2,1)} %w1_hbm.1, bf16[3072,768]{1,0:T(8,128)(2,1)} %w2_hbm.1, bf16[40,768]{1,0:T(8,128)(2,1)} %gout.1), custom_call_target="tpu_custom_call" | custom-call | flops 12079595520 | bytes 9437184 | tf_op jit(solution)/shard_map/pallas_call | solution.py:459
  125.8 1.7 %shard_map.60 = (f32[40,768]{1,0:T(8,128)}, f32[40,768]{1,0:T(8,128)}) custom-call(f32[40,768]{1,0:T(8,128)} %get-tuple-element.4.a, f32[40,768]{1,0:T(8,128)} %get-tuple-element.5.b), custom_call_target="tpu_custom_call" | custom-call | tf_op jit(solution)/shard_map/pallas_call | solution.py:470
